TPU v7x, 256 devices: a whole 4x4x8 slice. The times are simulated.
256 devices in a mesh: runs: 16 (over y, z_lo, core), blocks: 16 (over x, z_hi).
Axes of the slice: x: 4, y: 4, z: 8 (z_hi: 4, z_lo: 2; z = z_hi * 2 + z_lo), core: 2. Of those that a mesh axis runs over, the one named last changes fastest.
Arguments:
- signs: bfloat16 [16384, 49152], P('runs', 'blocks'), may hold values from -1 to 1, as said below
- targets: float32 [16384, 128], P('runs'), may hold values from -6 to 6
- weights: float32 [49152, 128], P('blocks'), may hold values from -6 to 6
Outputs:
- fitted: float32 [49152, 128], P('blocks')
- residual: float32 [16384, 128], P(('runs', 'blocks'))
Inputs may be any that keep to these rules, and one draw needn't show every extreme that they name: `signs`: every entry is +1 or -1.
All inputs are finite; a program needn't handle non-finite values.
Results may differ from a plain program's by a relative error of at most 0.004.
Values may be sent and summed in bfloat16 or wider, within the bound.
No kernel may reach another device: no remote copies, remote signals or barrier semaphores. Data moves between devices by JAX's collectives and lax.ppermute only.
A program may use at most 64 MiB of HBM per device.

v0:
```python
import math

import jax
import jax.numpy as jnp
from jax import lax
from jax.sharding import PartitionSpec as P

ITERS = 3


def shrink(moved, limit_value):
    return jnp.sign(moved) * jnp.maximum(jnp.abs(moved) - limit_value, 0.0)


def body(signs, targets, weights):
    run_dev = signs.shape[0]
    blk_dev = signs.shape[1]
    runs_count = lax.axis_size("runs")
    blocks_count = lax.axis_size("blocks")
    total_runs = run_dev * runs_count
    total_blocks = blk_dev * blocks_count
    scale_factor = 1.0 / math.sqrt(total_blocks)
    step_size = 1.0 / (1.0 + math.sqrt(total_runs / total_blocks)) ** 2
    limit_value = 0.5 * step_size
    run_share = run_dev // blocks_count
    first_row = lax.axis_index("blocks") * run_share
    fitted = weights
    residual_own = lax.dynamic_slice_in_dim(targets, first_row, run_share, 0)
    for turn in range(ITERS):
        weight_half = fitted.astype(jnp.bfloat16)
        partial_pred = jnp.dot(signs, weight_half, preferred_element_type=jnp.float32)
        predicted = lax.psum(partial_pred, "blocks") * scale_factor
        residual_full = predicted - targets
        residual_half = residual_full.astype(jnp.bfloat16)
        residual_own = lax.dynamic_slice_in_dim(residual_full, first_row, run_share, 0)
        partial_grad = lax.dot_general(
            signs, residual_half, (((0,), (0,)), ((), ())), preferred_element_type=jnp.float32
        )
        gradient = lax.psum(partial_grad, "runs") * scale_factor
        fitted = shrink(fitted - step_size * gradient, limit_value)
    return (fitted, residual_own)


def solution(mesh):
    in_specs = (P("runs", "blocks"), P("runs", None), P("blocks", None))
    out_specs = (P("blocks", None), P(("runs", "blocks"), None))
    return jax.shard_map(body, mesh=mesh, in_specs=in_specs, out_specs=out_specs, check_vma=False)
```

profile of v0, /device:TPU:1, one launch (start us, length us, event | category | flops | bytes accessed | tf_op | source)
XLA Modules:
  0.0 937.2 jit_solution(11958262523476699871)
XLA Ops:
  7.2 0.0 copy-start
  7.2 0.0 all-reduce.7.cloned.1.call-start
  7.2 6.2 fusion.2
  13.5 0.0 all-reduce.7.cloned.1.call-update
  13.5 0.0 all-reduce.9.cloned.1.call-start
  13.5 0.0 copy-done
  13.6 0.2 copy.5
  13.8 160.5 %all-reduce.7.cloned.1.call-done = f32[1024,128]{0,1:T(8,128)} async-done(((f32[1024,128]{0,1:T(8,128)}), f32[1024,128]{0,1:T(8,128)}) %all-reduce.7.cloned.1.call-update) | async-done | bytes 524304 | tf_op jit(solution)/shard_map/psum | solution.py:32
  174.3 5.1 convolution_bitcast_fusion.2
  179.4 0.0 all-reduce.9.cloned.1.call-update
  179.4 0.0 all-reduce.11.cloned.1.call-start
  179.5 1.9 copy.6
  181.3 132.3 %all-reduce.9.cloned.1.call-done = f32[3072,128]{0,1:T(8,128)} async-done(((f32[3072,128]{0,1:T(8,128)}), f32[3072,128]{0,1:T(8,128)}) %all-reduce.9.cloned.1.call-update) | async-done | bytes 1572880 | tf_op jit(solution)/shard_map/psum | solution.py:39
  313.6 6.4 convolution_bitcast_fusion.4
  320.0 0.0 all-reduce.11.cloned.1.call-update
  320.1 0.0 all-reduce.13.cloned.1.call-start
  320.1 157.6 %all-reduce.11.cloned.1.call-done = f32[1024,128]{0,1:T(8,128)} async-done(((f32[1024,128]{0,1:T(8,128)}), f32[1024,128]{0,1:T(8,128)}) %all-reduce.11.cloned.1.call-update) | async-done | bytes 524304 | tf_op jit(solution)/shard_map/psum | solution.py:32
  477.7 5.1 convolution_bitcast_fusion.1
  482.8 0.0 all-reduce.13.cloned.1.call-update
  482.8 0.0 all-reduce.15.cloned.1.call-start
  482.9 134.1 %all-reduce.13.cloned.1.call-done = f32[3072,128]{0,1:T(8,128)} async-done(((f32[3072,128]{0,1:T(8,128)}), f32[3072,128]{0,1:T(8,128)}) %all-reduce.13.cloned.1.call-update) | async-done | bytes 1572880 | tf_op jit(solution)/shard_map/psum | solution.py:39
  617.0 7.3 convolution_bitcast_fusion.3
  624.2 0.0 all-reduce.15.cloned.1.call-update
  624.3 0.2 all-reduce.17.cloned.1.call-start
  624.5 157.2 %all-reduce.15.cloned.1.call-done = f32[1024,128]{0,1:T(8,128)} async-done(((f32[1024,128]{0,1:T(8,128)}), f32[1024,128]{0,1:T(8,128)}) %all-reduce.15.cloned.1.call-update) | async-done | bytes 524304 | tf_op jit(solution)/shard_map/psum | solution.py:32
  781.7 1.1 multiply_subtract_fusion
  782.8 4.9 convolution_bitcast_fusion
  787.7 0.0 all-reduce.17.cloned.1.call-update
  787.8 0.1 constant_dynamic-slice_fusion
  787.8 0.7 copy.10
  788.5 133.3 %all-reduce.17.cloned.1.call-done = f32[3072,128]{0,1:T(8,128)} async-done(((f32[3072,128]{0,1:T(8,128)}), f32[3072,128]{0,1:T(8,128)}) %all-reduce.17.cloned.1.call-update) | async-done | bytes 1572880 | tf_op jit(solution)/shard_map/psum | solution.py:39
  921.9 5.5 maximum_multiply_fusion
  927.4 3.0 copy.9
Async XLA Ops:
  7.2 6.4 copy-start
  7.2 167.1 %all-reduce.7.cloned.1.call-start = ((), (), s32[]{:S(2)}) async-start(), calls=%async_computation | async-start | bytes 1048576 | tf_op jit(solution)/shard_map/psum | solution.py:32
  13.5 300.1 %all-reduce.9.cloned.1.call-start = ((), (), s32[]{:S(2)}) async-start(), calls=%async_computation.1 | async-start | bytes 3145728 | tf_op jit(solution)/shard_map/psum | solution.py:39
  179.4 298.2 %all-reduce.11.cloned.1.call-start = ((), (), s32[]{:S(2)}) async-start(), calls=%async_computation.2 | async-start | bytes 1048576 | tf_op jit(solution)/shard_map/psum | solution.py:32
  320.1 296.9 %all-reduce.13.cloned.1.call-start = ((), (), s32[]{:S(2)}) async-start(), calls=%async_computation.3 | async-start | bytes 3145728 | tf_op jit(solution)/shard_map/psum | solution.py:39
  482.8 298.9 %all-reduce.15.cloned.1.call-start = ((), (), s32[]{:S(2)}) async-start(), calls=%async_computation.4 | async-start | bytes 1048576 | tf_op jit(solution)/shard_map/psum | solution.py:32
  624.3 297.6 %all-reduce.17.cloned.1.call-start = ((), (), s32[]{:S(2)}) async-start(), calls=%async_computation.5 | async-start | bytes 3145728 | tf_op jit(solution)/shard_map/psum | solution.py:39
Sparse Core Ops, SparseCore 0:
  13.6 160.6 all-reduce.6
  179.5 134.0 all-reduce.8
  320.2 157.4 all-reduce.10
  482.9 133.9 all-reduce.12
  624.4 157.2 all-reduce.14
  787.9 133.9 all-reduce.16
where the time goes:
time: 937 us
  waiting for transfers between devices  875 us (93%)
  matrix products  35.1 us (4%)
  between operations  14.2 us (2%)
    psum x3, waiting for transfers between devices, body(): predicted = lax.psum(partial_pred, 'blocks') * scale_factor  475 us
    psum x3, waiting for transfers between devices, body(): gradient = lax.psum(partial_grad, 'runs') * scale_factor  400 us
    dot_general x3, matrix products, body(): jnp.dot(signs, weight_half, preferred_element_type=jnp.float32)  20 us
  transfers between devices with their start and end apart: 6, of which 6 were waited for; matrix products, arithmetic and copies ran while one was open for 0% of the time, Pallas kernels for 0%

commit v1 on v0

v1 whole, which is shorter than its diff:
```python
import math

import jax
import jax.numpy as jnp
from jax import lax
from jax.sharding import PartitionSpec as P

ITERS = 3


def shrink(moved, limit_value):
    return jnp.sign(moved) * jnp.maximum(jnp.abs(moved) - limit_value, 0.0)


def sum_share(partial, axis):
    parts = lax.axis_size(axis)
    rows = partial.shape[0] // parts
    pieces = partial.astype(jnp.bfloat16).reshape(parts, rows, partial.shape[1])
    pieces = lax.all_to_all(pieces, axis, 0, 0)
    return jnp.sum(pieces.astype(jnp.float32), axis=0)


def gather_shares(share, axis):
    parts = lax.axis_size(axis)
    pieces = jnp.broadcast_to(share[None], (parts,) + share.shape)
    pieces = lax.all_to_all(pieces, axis, 0, 0)
    return pieces.reshape(parts * share.shape[0], share.shape[1])


def body(signs, targets, weights):
    run_dev = signs.shape[0]
    blk_dev = signs.shape[1]
    runs_count = lax.axis_size("runs")
    blocks_count = lax.axis_size("blocks")
    total_runs = run_dev * runs_count
    total_blocks = blk_dev * blocks_count
    scale_factor = 1.0 / math.sqrt(total_blocks)
    step_size = 1.0 / (1.0 + math.sqrt(total_runs / total_blocks)) ** 2
    limit_value = 0.5 * step_size
    run_share = run_dev // blocks_count
    blk_share = blk_dev // runs_count
    targets_own = lax.dynamic_slice_in_dim(targets, lax.axis_index("blocks") * run_share, run_share, 0)
    fitted_own = lax.dynamic_slice_in_dim(weights, lax.axis_index("runs") * blk_share, blk_share, 0)
    weight_half = weights.astype(jnp.bfloat16)
    for turn in range(ITERS):
        partial_pred = jnp.dot(signs, weight_half, preferred_element_type=jnp.float32)
        residual_own = sum_share(partial_pred, "blocks") * scale_factor - targets_own
        residual_half = gather_shares(residual_own.astype(jnp.bfloat16), "blocks")
        partial_grad = lax.dot_general(
            signs, residual_half, (((0,), (0,)), ((), ())), preferred_element_type=jnp.float32
        )
        gradient_own = sum_share(partial_grad, "runs") * scale_factor
        fitted_own = shrink(fitted_own - step_size * gradient_own, limit_value)
        weight_half = gather_shares(fitted_own.astype(jnp.bfloat16), "runs")
    return (weight_half.astype(jnp.float32), residual_own)


def solution(mesh):
    in_specs = (P("runs", "blocks"), P("runs", None), P("blocks", None))
    out_specs = (P("blocks", None), P(("runs", "blocks"), None))
    return jax.shard_map(body, mesh=mesh, in_specs=in_specs, out_specs=out_specs, check_vma=False)
```

time: 937 us -> 242 us (0.26)
  waiting for transfers between devices: 875 us -> 25.4 us
  blocking collectives: 0 us -> 159 us
  starting transfers between devices: 0.43 us -> 20.2 us
  between operations: 14.2 us -> 0.78 us
    psum x6 -> x0, waiting for transfers between devices: 875 us -> none  [the longest x3 475 us: body(): predicted = lax.psum(partial_pred, 'blocks') * scale_factor]
    all_to_all x0 -> x10, blocking collectives: none -> 159 us  [the longest x6 91.2 us: gather_shares(): pieces = lax.all_to_all(pieces, axis, 0, 0)]
    all_to_all x0 -> x2, waiting for transfers between devices: none -> 25.4 us  [sum_share(): pieces = lax.all_to_all(pieces, axis, 0, 0)]
    all_to_all x0 -> x2, starting transfers between devices: none -> 20.2 us  [sum_share(): pieces = lax.all_to_all(pieces, axis, 0, 0)]
  transfers between devices with their start and end apart: 6 -> 2, of which waited for: 6 -> 2; matrix products, arithmetic and copies ran while one was open for 0% -> 0% of each run, Pallas kernels for 0% -> 0%
where the time goes in v1:
time: 242 us; the launch traced here: 241 us
  blocking collectives  159 us (66%)
  matrix products  27.2 us (11%)
  waiting for transfers between devices  25.4 us (10%)
  starting transfers between devices  20.2 us (8%)
  other arithmetic  5.77 us (2%)
  local copies, waits for them, and re-layouts  2.8 us (1%)
    all_to_all x6, blocking collectives, gather_shares(): pieces = lax.all_to_all(pieces, axis, 0, 0)  91.2 us
    all_to_all x4, blocking collectives, sum_share(): pieces = lax.all_to_all(pieces, axis, 0, 0)  67.7 us
    all_to_all x2, waiting for transfers between devices, sum_share(): pieces = lax.all_to_all(pieces, axis, 0, 0)  25.4 us
    all_to_all x2, starting transfers between devices, sum_share(): pieces = lax.all_to_all(pieces, axis, 0, 0)  20.2 us
    dot_general x3, matrix products, body(): jnp.dot(signs, weight_half, preferred_element_type=jnp.float32)  15.8 us
    dot_general x3, matrix products, body(): lax.dot_general(signs, residual_half, (((0,), (0,)), ((), ())), preferred...  11.4 us
  transfers between devices with their start and end apart: 2, of which 2 were waited for; matrix products, arithmetic and copies ran while one was open for 0% of the time, Pallas kernels for 0%

profile of v1, /device:TPU:1, one launch (start us, length us, event | category | flops | bytes accessed | tf_op | source)
XLA Modules:
  0.0 241.0 jit_solution(14267648718994947797)
XLA Ops:
  0.6 5.7 %convolution_convert_fusion.5 = bf16[1024,128]{1,0:T(8,128)(2,1)} fusion(bf16[1024,3072]{1,0:T(8,128)(2,1)} %param.3, f32[3072,128]{1,0:T(8,128)} %param.5), kind=kOutput, calls=%fused_computation.11 | convolution fusion | flops 805830656 | bytes 8126464 | tf_op jit(solution)/shard_map/dot_general | solution.py:46
  6.3 11.6 %all-to-all-start = ((bf16[16,64,128]{2,1,0:T(8,128)(2,1)}), bf16[16,64,128]{2,1,0:T(8,128)(2,1)S(1)}, u32[]{:S(2)}, u32[]{:S(2)}) async-start(bf16[16,64,128]{2,1,0:T(8,128)(2,1)} %bitcast), calls=%async_computation | async-start | bytes 524288 | tf_op jit(solution)/shard_map/all_to_all | solution.py:19
  17.9 12.4 %all-to-all-done = bf16[16,64,128]{2,1,0:T(8,128)(2,1)S(1)} async-done(((bf16[16,64,128]{2,1,0:T(8,128)(2,1)}), bf16[16,64,128]{2,1,0:T(8,128)(2,1)S(1)}, u32[]{:S(2)}, u32[]{:S(2)}) %all-to-all-start) | async-done | bytes 262176 | tf_op jit(solution)/shard_map/all_to_all | solution.py:19
  30.4 0.8 subtract_convert_fusion.1
  31.2 13.3 %all_to_all.60 = bf16[16,64,128]{2,1,0:T(8,128)(2,1)S(1)} all-to-all(bf16[16,64,128]{2,1,0:T(8,128)(2,1)S(1)} %broadcast_in_dim.12), channel_id=1, replica_groups=mesh['runs'=16,'blocks'=16] {'blocks'}, dimensions={0} | all-to-all | bytes 524288 | tf_op jit(solution)/shard_map/all_to_all | solution.py:26
  44.5 3.8 %fusion = bf16[3072,128]{0,1:T(8,128)(2,1)S(1)} fusion(bf16[1024,128]{1,0:T(8,128)(2,1)S(1)} %bitcast.39, bf16[1024,3072]{1,0:T(8,128)(2,1)} %param.3), kind=kOutput, calls=%fused_computation.3 | convolution fusion | flops 805699584 | bytes 7340032 | tf_op jit(solution)/shard_map/dot_general | solution.py:49
  48.3 1.2 copy.5
  49.5 8.6 %all-to-all-start.2 = ((bf16[16,192,128]{2,1,0:T(8,128)(2,1)}), bf16[16,192,128]{2,1,0:T(8,128)(2,1)S(1)}, u32[]{:S(2)}, u32[]{:S(2)}) async-start(bf16[16,192,128]{2,1,0:T(8,128)(2,1)} %bitcast.3), calls=%async_computation.2 | async-start | bytes 1572864 | tf_op jit(solution)/shard_map/all_to_all | solution.py:19
  58.1 13.0 %all-to-all-done.2 = bf16[16,192,128]{2,1,0:T(8,128)(2,1)S(1)} async-done(((bf16[16,192,128]{2,1,0:T(8,128)(2,1)}), bf16[16,192,128]{2,1,0:T(8,128)(2,1)S(1)}, u32[]{:S(2)}, u32[]{:S(2)}) %all-to-all-start.2) | async-done | bytes 786464 | tf_op jit(solution)/shard_map/all_to_all | solution.py:19
  71.1 0.1 convert_reduce_fusion.2
  71.2 0.9 fusion.8
  72.1 0.1 broadcast_in_dim.13
  72.3 16.1 %all_to_all.61 = bf16[16,192,128]{2,1,0:T(8,128)(2,1)S(1)} all-to-all(bf16[16,192,128]{2,1,0:T(8,128)(2,1)S(1)} %broadcast_in_dim.13), channel_id=1, replica_groups=mesh['runs'=16,'blocks'=16] {'runs'}, dimensions={0} | all-to-all | bytes 1572864 | tf_op jit(solution)/shard_map/all_to_all | solution.py:26
  88.4 5.0 %fusion.3 = bf16[1024,128]{0,1:T(8,128)(2,1)S(1)} fusion(bf16[3072,128]{1,0:T(8,128)(2,1)S(1)} %bitcast.35, bf16[1024,3072]{1,0:T(8,128)(2,1)} %param.3), kind=kOutput, calls=%fused_computation.12 | convolution fusion | flops 805437440 | bytes 7340032 | tf_op jit(solution)/shard_map/dot_general | solution.py:46
  93.5 0.2 copy.6
  93.6 14.0 %all_to_all.62 = bf16[16,64,128]{2,1,0:T(8,128)(2,1)S(1)} all-to-all(bf16[16,64,128]{2,1,0:T(8,128)(2,1)S(1)} %bitcast.42), channel_id=1, replica_groups=mesh['runs'=16,'blocks'=16] {'blocks'}, dimensions={0} | all-to-all | bytes 524288 | tf_op jit(solution)/shard_map/all_to_all | solution.py:19
  107.7 0.8 subtract_convert_fusion
  108.5 14.6 %all_to_all.63 = bf16[16,64,128]{2,1,0:T(8,128)(2,1)S(1)} all-to-all(bf16[16,64,128]{2,1,0:T(8,128)(2,1)S(1)} %broadcast_in_dim.14), channel_id=1, replica_groups=mesh['runs'=16,'blocks'=16] {'blocks'}, dimensions={0} | all-to-all | bytes 524288 | tf_op jit(solution)/shard_map/all_to_all | solution.py:26
  123.1 3.8 %fusion.1 = bf16[3072,128]{0,1:T(8,128)(2,1)S(1)} fusion(bf16[1024,128]{1,0:T(8,128)(2,1)S(1)} %bitcast.40, bf16[1024,3072]{1,0:T(8,128)(2,1)} %param.3), kind=kOutput, calls=%fused_computation.4 | convolution fusion | flops 805699584 | bytes 7340032 | tf_op jit(solution)/shard_map/dot_general | solution.py:49
  126.9 0.4 copy.7
  127.3 19.9 %all_to_all.64 = bf16[16,192,128]{2,1,0:T(8,128)(2,1)S(1)} all-to-all(bf16[16,192,128]{2,1,0:T(8,128)(2,1)S(1)} %bitcast.37), channel_id=1, replica_groups=mesh['runs'=16,'blocks'=16] {'runs'}, dimensions={0} | all-to-all | bytes 1572864 | tf_op jit(solution)/shard_map/all_to_all | solution.py:19
  147.2 0.1 convert_reduce_fusion.1
  147.3 0.1 fusion.6
  147.3 0.1 broadcast_in_dim.15
  147.5 16.2 %all_to_all.65 = bf16[16,192,128]{2,1,0:T(8,128)(2,1)S(1)} all-to-all(bf16[16,192,128]{2,1,0:T(8,128)(2,1)S(1)} %broadcast_in_dim.15), channel_id=1, replica_groups=mesh['runs'=16,'blocks'=16] {'runs'}, dimensions={0} | all-to-all | bytes 1572864 | tf_op jit(solution)/shard_map/all_to_all | solution.py:26
  163.8 5.0 %fusion.4 = bf16[1024,128]{0,1:T(8,128)(2,1)S(1)} fusion(bf16[3072,128]{1,0:T(8,128)(2,1)S(1)} %bitcast.36, bf16[1024,3072]{1,0:T(8,128)(2,1)} %param.3), kind=kOutput, calls=%fused_computation.13 | convolution fusion | flops 805437440 | bytes 7340032 | tf_op jit(solution)/shard_map/dot_general | solution.py:46
  168.8 0.2 copy.8
  169.0 14.0 %all_to_all.66 = bf16[16,64,128]{2,1,0:T(8,128)(2,1)S(1)} all-to-all(bf16[16,64,128]{2,1,0:T(8,128)(2,1)S(1)} %bitcast.43), channel_id=1, replica_groups=mesh['runs'=16,'blocks'=16] {'blocks'}, dimensions={0} | all-to-all | bytes 524288 | tf_op jit(solution)/shard_map/all_to_all | solution.py:19
  183.0 1.4 fusion.7
  184.4 14.6 %all_to_all.67 = bf16[16,64,128]{2,1,0:T(8,128)(2,1)S(1)} all-to-all(bf16[16,64,128]{2,1,0:T(8,128)(2,1)S(1)} %broadcast_in_dim.16), channel_id=1, replica_groups=mesh['runs'=16,'blocks'=16] {'blocks'}, dimensions={0} | all-to-all | bytes 524288 | tf_op jit(solution)/shard_map/all_to_all | solution.py:26
  199.0 3.8 %fusion.2 = bf16[3072,128]{0,1:T(8,128)(2,1)S(1)} fusion(bf16[1024,128]{1,0:T(8,128)(2,1)S(1)} %bitcast.41, bf16[1024,3072]{1,0:T(8,128)(2,1)} %param.3), kind=kOutput, calls=%fused_computation.5 | convolution fusion | flops 805699584 | bytes 7340032 | tf_op jit(solution)/shard_map/dot_general | solution.py:49
  202.9 0.4 copy.9
  203.2 19.9 %all_to_all.68 = bf16[16,192,128]{2,1,0:T(8,128)(2,1)S(1)} all-to-all(bf16[16,192,128]{2,1,0:T(8,128)(2,1)S(1)} %bitcast.38), channel_id=1, replica_groups=mesh['runs'=16,'blocks'=16] {'runs'}, dimensions={0} | all-to-all | bytes 1572864 | tf_op jit(solution)/shard_map/all_to_all | solution.py:19
  223.1 0.1 convert_reduce_fusion
  223.2 0.1 multiply_convert_fusion
  223.3 0.1 broadcast_in_dim.17
  223.5 16.2 %all_to_all.69 = bf16[16,192,128]{2,1,0:T(8,128)(2,1)S(1)} all-to-all(bf16[16,192,128]{2,1,0:T(8,128)(2,1)S(1)} %broadcast_in_dim.17), channel_id=1, replica_groups=mesh['runs'=16,'blocks'=16] {'runs'}, dimensions={0} | all-to-all | bytes 1572864 | tf_op jit(solution)/shard_map/all_to_all | solution.py:26
  239.7 1.3 bitcast_convert_fusion
  (6 shorter events, 0.3 us)
Async XLA Ops:
  6.3 24.0 %all-to-all-start = ((bf16[16,64,128]{2,1,0:T(8,128)(2,1)}), bf16[16,64,128]{2,1,0:T(8,128)(2,1)S(1)}, u32[]{:S(2)}, u32[]{:S(2)}) async-start(bf16[16,64,128]{2,1,0:T(8,128)(2,1)} %bitcast), calls=%async_computation | async-start | bytes 524288 | tf_op jit(solution)/shard_map/all_to_all | solution.py:19
  49.5 21.6 %all-to-all-start.2 = ((bf16[16,192,128]{2,1,0:T(8,128)(2,1)}), bf16[16,192,128]{2,1,0:T(8,128)(2,1)S(1)}, u32[]{:S(2)}, u32[]{:S(2)}) async-start(bf16[16,192,128]{2,1,0:T(8,128)(2,1)} %bitcast.3), calls=%async_computation.2 | async-start | bytes 1572864 | tf_op jit(solution)/shard_map/all_to_all | solution.py:19
